TPU v7x, 512 devices: a whole 4x8x8 slice. The times are simulated.
512 devices in a mesh: seq: 128 (over y, z_lo, x), mp: 4 (over z_hi, core).
Axes of the slice: x: 4, y: 8, z: 8 (z_hi: 2, z_lo: 4; z = z_hi * 4 + z_lo), core: 2. Of those that a mesh axis runs over, the one named last changes fastest.
Arguments:
- state: bfloat16 [61440, 1024], P('seq'), may hold values from -60 to 60
- condition: bfloat16 [61440, 1024], P('seq'), may hold values from -6 to 6
- time_vector: bfloat16 [1024], replicated, may hold values from -4 to 4
- norm_gain: bfloat16 [1024], replicated, may hold values from 0.59765625 to 1.3984375
- w_qkv: bfloat16 [3, 1024, 1024], P(None, None, 'mp'), may hold values from -2 to 2
- w_out: bfloat16 [1024, 1024], P('mp'), may hold values from -0.75 to 0.75
- utterance_ids: int32 [61440], P('seq'), may hold values from 0 to 239, never falling along the last dimension, each value on 1 to 1024 neighbouring positions
Outputs:
- final_state: bfloat16 [61440, 1024], P('seq', 'mp')
Inputs may be any that keep to these rules, and one draw needn't show every extreme that they name: `utterance_ids`: never falling along the frames; each utterance has 1 to 1024 frames and one has exactly 1024.
All inputs are finite; a program needn't handle non-finite values.
Results may differ from a plain program's by a relative error of at most 0.03.
Values may be sent and summed in bfloat16 or wider, within the bound.
A program may use at most 64 MiB of HBM per device.

v0:
```python
import jax
import jax.numpy as jnp
from jax import lax
from jax.sharding import PartitionSpec as P

HEAD_DIM = 64
BLOCK = 24


def shifted(shard, axis, by):
    count = lax.axis_size(axis)
    pairs = [(i, i + by) for i in range(count) if 0 <= i + by < count]
    return lax.ppermute(shard, axis, pairs)


def banded_attention(q, keys_values, seg_ext, seg_plus, head_dim):
    frames = q.shape[0]
    width = q.shape[1]
    nblocks = frames // BLOCK
    heads = width // head_dim
    rows = (jnp.arange(nblocks, dtype=jnp.int32) * BLOCK)[:, None] + jnp.arange(
        4 * BLOCK, dtype=jnp.int32
    )[None, :]
    window = keys_values[rows]
    k_rows = window[:, :, :width].reshape(nblocks, 4 * BLOCK, heads, head_dim)
    v_rows = window[:, :, width:].reshape(nblocks, 4 * BLOCK, heads, head_dim)
    q_rows = q.reshape(nblocks, BLOCK, heads, head_dim)
    scores = (
        jnp.einsum("bqhe,bkhe->bhqk", q_rows, k_rows, preferred_element_type=jnp.float32) * 0.125
    )
    k_seg = seg_ext[rows]
    q_seg = seg_plus.reshape(nblocks, BLOCK)
    allowed = (q_seg[:, :, None] == k_seg[:, None, :])[:, None]
    scores = jnp.where(allowed, scores, -1e30)
    top = jnp.max(scores, axis=-1, keepdims=True)
    expo = jnp.exp(scores - top)
    probs = (expo / jnp.sum(expo, axis=-1, keepdims=True)).astype(jnp.bfloat16)
    out = jnp.einsum("bhqk,bkhe->bqhe", probs, v_rows, preferred_element_type=jnp.float32)
    return out.astype(jnp.bfloat16).reshape(frames, width)


def velocity_terms(x_full, condition, time_vector, norm_gain, w_qkv, w_out, seg_ext, seg_plus, t):
    h = x_full + condition.astype(jnp.float32) + t * time_vector.astype(jnp.float32)
    scale = lax.rsqrt(jnp.mean(h * h, axis=-1, keepdims=True) + 1e-06)
    normed = (h * scale * norm_gain.astype(jnp.float32)).astype(jnp.bfloat16)
    q = jnp.dot(normed, w_qkv[0], preferred_element_type=jnp.float32).astype(jnp.bfloat16)
    k = jnp.dot(normed, w_qkv[1], preferred_element_type=jnp.float32).astype(jnp.bfloat16)
    v = jnp.dot(normed, w_qkv[2], preferred_element_type=jnp.float32).astype(jnp.bfloat16)
    joined = jnp.concatenate([k, v], axis=1)
    behind = shifted(joined[-2 * BLOCK :], "seq", 1)
    before = shifted(joined[:BLOCK], "seq", -1)
    keys_values = jnp.concatenate([behind, joined, before], axis=0)
    attended = banded_attention(q, keys_values, seg_ext, seg_plus, HEAD_DIM)
    return jnp.dot(attended, w_out, preferred_element_type=jnp.float32)


def shards(state, condition, time_vector, norm_gain, w_qkv, w_out, utterance_ids):
    seg_plus = utterance_ids + 1
    seg_behind = shifted(seg_plus[-2 * BLOCK :], "seq", 1)
    seg_before = shifted(seg_plus[:BLOCK], "seq", -1)
    seg_ext = jnp.concatenate([seg_behind, seg_plus, seg_before], axis=0)
    x_full = state.astype(jnp.float32)
    parts = lax.axis_size("mp")
    share = x_full.shape[1] // parts
    for step in range(2):
        terms = velocity_terms(
            x_full, condition, time_vector, norm_gain, w_qkv, w_out, seg_ext, seg_plus, 0.5 * step
        )
        total = lax.psum(terms.astype(jnp.bfloat16), "mp").astype(jnp.float32)
        x_full = x_full + 0.5 * total
    mine = lax.dynamic_slice_in_dim(x_full, lax.axis_index("mp") * share, share, 1)
    return mine.astype(jnp.bfloat16)


def solution(mesh):
    in_specs = (
        P("seq", None),
        P("seq", None),
        P(),
        P(),
        P(None, None, "mp"),
        P("mp", None),
        P("seq"),
    )
    out_specs = P("seq", "mp")
    return jax.shard_map(shards, mesh=mesh, in_specs=in_specs, out_specs=out_specs, check_vma=False)
```

profile of v0, /device:TPU:1, one launch (start us, length us, event | category | flops | bytes accessed | tf_op | source)
XLA Modules:
  0.0 267.9 jit_solution(17091238557710755683)
XLA Ops:
  6.5 0.8 broadcast_add_fusion
  7.5 3.9 %collective-permute-start.2 = (s32[48]{0:T(128)S(1)}, s32[48]{0:T(128)S(1)}, u32[]{:S(2)}, u32[]{:S(2)}) collective-permute-start(s32[48]{0:T(128)S(1)} %slice.47), channel_id=1, source_target_pairs={{0,4},{4,8},{8,12},{12,16},{16,20},{20,24},{24,28},{28,32},{32,36}... | collective-permute-start | bytes 584 | tf_op jit(solution)/shard_map/ppermute | solution.py:13
  11.4 1.3 collective-permute-start.3
  12.7 0.7 convert_element_type.75
  13.4 1.3 convert_multiply_fusion
  14.7 2.0 multiply_reduce_fusion.1
  16.7 0.4 multiply_convert_fusion.1
  17.1 0.9 copy-done.11
  18.0 0.4 convolution_convert_fusion.8
  18.5 0.4 convolution_convert_fusion.9
  18.9 1.3 collective-permute-start.1
  20.2 5.2 %collective-permute-start = (bf16[48,512]{1,0:T(8,128)(2,1)S(1)}, bf16[48,512]{1,0:T(8,128)(2,1)}, u32[]{:S(2)}, u32[]{:S(2)}) collective-permute-start(bf16[48,512]{1,0:T(8,128)(2,1)S(1)} %pad_maximum_fusion.3), channel_id=1, source_target_pairs={{0,4},{4,8},{8,12},{12,16},{16,20},{20,24},{24,28},{28,32},{32,36}... | collective-permute-start | bytes 147464 | tf_op jit(solution)/shard_map/ppermute | solution.py:13
  25.5 0.4 convolution_convert_fusion.7
  26.1 1.0 reshape.94
  27.3 7.2 %gather_fusion.1 = s32[1920]{0:T(1024)S(1)} fusion(s32[552]{0:T(1024)S(1)} %pad_add_fusion, s32[2048]{0:T(1024)S(1)} %pad_clamp_fusion), kind=kCustom, calls=%fused_computation.1 | custom fusion | bytes 23040 | tf_op jit(solution)/shard_map/gather | solution.py:31
  34.6 0.8 broadcast_compare_fusion
  35.3 0.6 copy-done.10
  35.9 0.9 pad_maximum_fusion
  36.8 6.8 %gather_fusion = bf16[1920,512]{1,0:T(8,128)(2,1)} fusion(bf16[552,512]{1,0:T(8,128)(2,1)S(1)} %pad_maximum_fusion, s32[2048]{0:T(1024)S(1)} %pad_clamp_fusion), kind=kCustom, calls=%fused_computation | custom fusion | bytes 3939840 | tf_op jit(solution)/shard_map/gather | solution.py:24
  43.6 2.6 fusion.32
  46.1 2.4 copy.23
  48.5 2.9 %fusion.9 = f32[20,4,24,96]{3,2,1,0:T(8,128)} fusion(bf16[20,96,4,64]{1,3,2,0:T(8,128)(2,1)} %bitcast.48, bf16[20,24,4,64]{3,2,1,0:T(4,128)(2,1)} %reshape.94, pred[20,24,96]{2,1,0:T(8,128)(4,1)S(1)} %copy-done.6), kind=kOutput, calls=%fused_computation.23 | convolution fusion | flops 23961600 | bytes 2012160 | tf_op jit(solution)/shard_map/bqhe,bkhe->bhqk/dot_general | solution.py:29
  51.5 2.7 %fusion.33 = f32[20,4,24]{2,1,0:T(4,128)} fusion(f32[20,4,24,96]{3,2,1,0:T(8,128)} %fusion.9), kind=kOutput, calls=%fused_computation.74 | output fusion | flops 368735 | bytes 744960 | tf_op jit(solution)/shard_map/sub | solution.py:36
  54.2 1.4 copy.22
  55.6 5.4 %fusion.10 = bf16[20,24,4,64]{3,1,2,0:T(8,128)(2,1)S(1)} fusion(bf16[20,96,4,64]{1,3,2,0:T(8,128)(2,1)} %bitcast.49, f32[20,4,24]{2,1,0:T(4,128)} %fusion.33, f32[20,4,24,96]{3,2,1,0:T(8,128)} %fusion.9), kind=kOutput, calls=%fused_computation.26 | convolution fusion | flops 24270816 | bytes 1973760 | tf_op jit(solution)/shard_map/bhqk,bkhe->bqhe/dot_general | solution.py:38
  61.2 0.3 reshape.96
  61.6 1.4 convolution_convert_fusion.1
  63.0 85.0 %all-reduce.3.cloned.1.call-done = bf16[480,1024]{1,0:T(8,128)(2,1)} async-done(((bf16[480,1024]{1,0:T(8,128)(2,1)}), bf16[480,1024]{1,0:T(8,128)(2,1)}) %all-reduce.3.cloned.1.call-update) | async-done | bytes 983056 | tf_op jit(solution)/shard_map/psum | solution.py:69
  148.1 1.9 multiply_reduce_fusion
  150.0 1.9 multiply_convert_fusion
  151.9 0.4 convolution_convert_fusion.5
  152.4 0.4 convolution_convert_fusion.6
  152.8 1.3 collective-permute-start.5
  154.1 4.2 %collective-permute-start.4 = (bf16[48,512]{1,0:T(8,128)(2,1)S(1)}, bf16[48,512]{1,0:T(8,128)(2,1)S(1)}, u32[]{:S(2)}, u32[]{:S(2)}) collective-permute-start(bf16[48,512]{1,0:T(8,128)(2,1)S(1)} %pad_maximum_fusion.2), channel_id=1, source_target_pairs={{0,4},{4,8},{8,12},{12,16},{16,20},{20,24},{24,28},{28,32},{32,36}... | collective-permute-start | bytes 147464 | tf_op jit(solution)/shard_map/ppermute | solution.py:13
  158.3 0.4 convolution_convert_fusion.4
  158.7 1.0 reshape.98
  159.8 6.4 %gather_fusion.2 = bf16[1920,512]{1,0:T(8,128)(2,1)S(1)} fusion(bf16[552,512]{1,0:T(8,128)(2,1)S(1)} %pad_maximum_fusion.1, s32[2048]{0:T(1024)S(1)} %pad_clamp_fusion), kind=kCustom, calls=%fused_computation.2 | custom fusion | bytes 3939840 | tf_op jit(solution)/shard_map/gather | solution.py:24
  166.2 1.2 fusion.31
  167.4 1.8 copy.25
  169.2 0.5 fusion.8
  169.7 1.0 copy-done.4
  170.7 0.6 fusion.34
  171.3 0.8 copy.24
  172.1 5.0 %fusion.11 = bf16[20,24,4,64]{3,1,2,0:T(8,128)(2,1)S(1)} fusion(bf16[20,96,4,64]{1,3,2,0:T(8,128)(2,1)S(1)} %bitcast.50, f32[20,4,24]{2,1,0:T(4,128)S(1)} %fusion.34, f32[20,4,24,96]{3,2,1,0:T(8,128)} %copy-done.4), kind=kOutput, calls=%fused_computation.27 | convolution fusion | flops 24270816 | bytes 1973760 | tf_op jit(solution)/shard_map/bhqk,bkhe->bqhe/dot_general | solution.py:38
  177.3 0.3 reshape.100
  177.6 1.4 convolution_convert_fusion
  179.0 80.2 %all-reduce.5.cloned.1.call-done = bf16[480,1024]{1,0:T(8,128)(2,1)} async-done(((bf16[480,1024]{1,0:T(8,128)(2,1)}), bf16[480,1024]{1,0:T(8,128)(2,1)}) %all-reduce.5.cloned.1.call-update) | async-done | bytes 983056 | tf_op jit(solution)/shard_map/psum | solution.py:69
  259.2 1.8 fusion.18
  (51 shorter events, 1.1 us)
Async XLA Ops:
  6.5 55.0 %copy-start = (bf16[256,1024]{1,0:T(8,128)(2,1)S(1)}, bf16[256,1024]{1,0:T(8,128)(2,1)}, u32[]{:S(2)}) copy-start(bf16[256,1024]{1,0:T(8,128)(2,1)} %param.12) | copy-start | bytes 1572868
  6.5 10.1 %copy-start.1 = (bf16[480,1024]{1,0:T(8,128)(2,1)S(1)}, bf16[480,1024]{1,0:T(8,128)(2,1)}, u32[]{:S(2)}) copy-start(bf16[480,1024]{1,0:T(8,128)(2,1)} %param.8) | copy-start | bytes 2949124
  6.5 10.1 %copy-start.2 = (bf16[480,1024]{1,0:T(8,128)(2,1)S(1)}, bf16[480,1024]{1,0:T(8,128)(2,1)}, u32[]{:S(2)}) copy-start(bf16[480,1024]{1,0:T(8,128)(2,1)} %param.7) | copy-start | bytes 2949124
  6.5 141.5 %all-reduce.3.cloned.1.call-start = ((), (), s32[]{:S(2)}) async-start(), calls=%async_computation | async-start | bytes 1966080 | tf_op jit(solution)/shard_map/psum | solution.py:69
  7.5 19.7 %collective-permute-start.2 = (s32[48]{0:T(128)S(1)}, s32[48]{0:T(128)S(1)}, u32[]{:S(2)}, u32[]{:S(2)}) collective-permute-start(s32[48]{0:T(128)S(1)} %slice.47), channel_id=1, source_target_pairs={{0,4},{4,8},{8,12},{12,16},{16,20},{20,24},{24,28},{28,32},{32,36}... | collective-permute-start | bytes 584 | tf_op jit(solution)/shard_map/ppermute | solution.py:13
  11.4 15.8 %collective-permute-start.3 = (s32[24]{0:T(128)S(1)}, s32[24]{0:T(128)S(1)}, u32[]{:S(2)}, u32[]{:S(2)}) collective-permute-start(s32[24]{0:T(128)S(1)} %slice.48), channel_id=1, source_target_pairs={{4,0},{8,4},{12,8},{16,12},{20,16},{24,20},{28,24},{32,28},{36,32}... | collective-permute-start | bytes 296 | tf_op jit(solution)/shard_map/ppermute | solution.py:13
  13.4 3.7 %copy-start.7 = (f32[1024]{0:T(1024)}, f32[1024]{0:T(1024)S(1)}, u32[]{:S(2)}) copy-start(f32[1024]{0:T(1024)S(1)} %convert_element_type.75) | copy-start | bytes 12292
  16.6 1.4 copy-start.11
  18.9 16.4 %collective-permute-start.1 = (bf16[24,512]{1,0:T(8,128)(2,1)S(1)}, bf16[24,512]{1,0:T(8,128)(2,1)S(1)}, u32[]{:S(2)}, u32[]{:S(2)}) collective-permute-start(bf16[24,512]{1,0:T(8,128)(2,1)S(1)} %pad_maximum_fusion.5), channel_id=1, source_target_pairs={{4,0},{8,4},{12,8},{16,12},{20,16},{24,20},{28,24},{32,28},{36,32}... | collective-permute-start | bytes 73736 | tf_op jit(solution)/shard_map/ppermute | solution.py:13
  20.2 15.7 %collective-permute-start = (bf16[48,512]{1,0:T(8,128)(2,1)S(1)}, bf16[48,512]{1,0:T(8,128)(2,1)}, u32[]{:S(2)}, u32[]{:S(2)}) collective-permute-start(bf16[48,512]{1,0:T(8,128)(2,1)S(1)} %pad_maximum_fusion.3), channel_id=1, source_target_pairs={{0,4},{4,8},{8,12},{12,16},{16,20},{20,24},{24,28},{28,32},{32,36}... | collective-permute-start | bytes 147464 | tf_op jit(solution)/shard_map/ppermute | solution.py:13
  35.3 0.6 copy-start.10
  46.1 2.4 copy-start.6
  61.2 86.8 %copy-start.9 = (f32[1024]{0:T(1024)S(1)}, f32[1024]{0:T(1024)}, u32[]{:S(2)}) copy-start(f32[1024]{0:T(1024)} %get-tuple-element.11) | copy-start | bytes 12292
  63.0 87.0 %copy-start.8 = (f32[1024]{0:T(1024)S(1)}, f32[1024]{0:T(1024)}, u32[]{:S(2)}) copy-start(f32[1024]{0:T(1024)} %copy-done.7) | copy-start | bytes 12292
  63.0 196.2 %all-reduce.5.cloned.1.call-start = ((), (), s32[]{:S(2)}) async-start(), calls=%async_computation.1 | async-start | bytes 1966080 | tf_op jit(solution)/shard_map/psum | solution.py:69
  148.1 2.0 copy-start.3
  150.0 1.9 copy-start.12
  152.8 6.9 %collective-permute-start.5 = (bf16[24,512]{1,0:T(8,128)(2,1)S(1)}, bf16[24,512]{1,0:T(8,128)(2,1)S(1)}, u32[]{:S(2)}, u32[]{:S(2)}) collective-permute-start(bf16[24,512]{1,0:T(8,128)(2,1)S(1)} %pad_maximum_fusion.4), channel_id=1, source_target_pairs={{4,0},{8,4},{12,8},{16,12},{20,16},{24,20},{28,24},{32,28},{36,32}... | collective-permute-start | bytes 73736 | tf_op jit(solution)/shard_map/ppermute | solution.py:13
  154.1 5.6 %collective-permute-start.4 = (bf16[48,512]{1,0:T(8,128)(2,1)S(1)}, bf16[48,512]{1,0:T(8,128)(2,1)S(1)}, u32[]{:S(2)}, u32[]{:S(2)}) collective-permute-start(bf16[48,512]{1,0:T(8,128)(2,1)S(1)} %pad_maximum_fusion.2), channel_id=1, source_target_pairs={{0,4},{4,8},{8,12},{12,16},{16,20},{20,24},{24,28},{28,32},{32,36}... | collective-permute-start | bytes 147464 | tf_op jit(solution)/shard_map/ppermute | solution.py:13
  167.4 1.8 copy-start.5
  169.7 1.0 copy-start.4
Sparse Core Ops, SparseCore 0:
  63.1 84.8 all-reduce.2
  179.1 80.0 all-reduce.4
where the time goes:
time: 269 us; the launch traced here: 268 us
  waiting for transfers between devices  165 us (61%)
  local copies, waits for them, and re-layouts  36.5 us (14%)
  matrix products  19.1 us (7%)
  starting transfers between devices  17.3 us (6%)
  other arithmetic  16.1 us (6%)
  between operations  13.7 us (5%)
    psum x2, waiting for transfers between devices, shards(): total = lax.psum(terms.astype(jnp.bfloat16), 'mp').astype(jnp.float32)  165 us
    ppermute x6, starting transfers between devices, shifted(): return lax.ppermute(shard, axis, pairs)  17.2 us
    gather x2, local copies, waits for them, and re-layouts, banded_attention(): window = keys_values[rows]  13.2 us
    dot_general x2, matrix products, banded_attention(): jnp.einsum('bhqk,bkhe->bqhe', probs, v_rows, preferred_element_type=jnp.f...  10.4 us
    unnamed x30, local copies, waits for them, and re-layouts  8.9 us
    gather x2, local copies, waits for them, and re-layouts, banded_attention(): k_seg = seg_ext[rows]  7.29 us
  transfers between devices with their start and end apart: 8, of which 2 were waited for; matrix products, arithmetic and copies ran while one was open for 6% of the time, Pallas kernels for 0%

commit v1 on v0

v1 whole, which is shorter than its diff:
```python
import jax
import jax.numpy as jnp
from jax import lax
from jax.experimental import pallas as pl
from jax.experimental.pallas import tpu as pltpu
from jax.sharding import PartitionSpec as P

MESH = pl.DeviceIdType.MESH
BF16 = jnp.bfloat16
F32 = jnp.float32

D = 1024
BLOCK = 24
ROWS = 480
EXT = 560
OWN = 48
TILE = 48
KEYS = 128
TILES = ROWS // TILE
LANES = 640
CHUNK = 96
CHUNKS = ROWS // CHUNK
BOUNDARY_FIRST = (0, CHUNKS - 1) + tuple(range(1, CHUNKS - 1))
PARTS = 8


def kernel(
    state_h, cond_h, wqkv_h, wout_h, tvec, gain, ids, out,
    st, cd, wq, wo, fq, fo, n1, n2, ids_prev, ids_next, bias, qa, qb, k, v, att, acc,
    pv_out, pv_in, x1, fin_out, fin_in,
    load_sem, zs, zr, xs, xr, ys, yr, hs, hr, ds, dr,
):
    seq = lax.axis_index("seq")
    mp = lax.axis_index("mp")
    x = seq % 4
    y = seq // 16
    odd = y % 2
    zh = mp // 2
    core = mp % 2
    part = x + 4 * odd

    at_z = (seq, (1 - zh) * 2 + core)
    at_x = [(seq - x + (x + hop) % 4, mp) for hop in (1, 2, 3)]
    sides = [1 - 2 * odd, 2 * odd - 1]
    at_y = [((seq + 16 * side + 128) % 128, mp) for side in sides]
    before = ((seq + 127) % 128, mp)
    after = ((seq + 1) % 128, mp)
    twin = (seq, zh * 2 + 1 - core)

    barrier = pltpu.get_barrier_semaphore()
    partners = [at_z] + at_x + at_y + [before, after, twin]
    for device in partners:
        pl.semaphore_signal(barrier, inc=1, device_id=device, device_id_type=MESH)

    loads = [
        pltpu.make_async_copy(src, dst, load_sem.at[i])
        for i, (src, dst) in enumerate(((state_h, st), (cond_h, cd), (wqkv_h, wq), (wout_h, wo)))
    ]
    for load in loads:
        load.start()

    def remote(src, dst, send, recv, device):
        return pltpu.make_async_remote_copy(
            src_ref=src, dst_ref=dst, send_sem=send, recv_sem=recv, device_id=device, device_id_type=MESH
        )

    def piece(pair, s, first, count=1):
        if s < 6:
            return pair[0].at[s // 2, pl.ds(512 * (s % 2) + 64 * first, 64 * count)]
        return pair[1].at[pl.ds(128 * (s % 2) + 16 * first, 16 * count)]

    mine, foreign = (wq, wo), (fq, fo)

    def z_copy(s):
        return remote(piece(mine, s, part), piece(foreign, s, part), zs.at[s], zr.at[s], at_z)

    def x_copy(s, hop):
        i = 3 * s + hop
        return remote(piece(foreign, s, part), piece(foreign, s, part), xs.at[i], xr.at[i], at_x[hop])

    def x_arrival(s, hop):
        other = (x + 3 - hop) % 4 + 4 * odd
        i = 3 * s + hop
        return remote(piece(foreign, s, other), piece(foreign, s, other), xs.at[i], xr.at[i], at_x[hop])

    def y_copy(s):
        block = piece(foreign, s, 4 * odd, 4)
        return remote(block, block, ys.at[s], yr.at[s], at_y[s % 2])

    def y_arrival(s):
        block = piece(foreign, s, 4 * (1 - odd), 4)
        return remote(block, block, ys.at[s], yr.at[s], at_y[s % 2])

    def tick_z(s):
        z_copy(s).wait_recv()
        for hop in range(3):
            x_copy(s, hop).start()

    def tick_x(s):
        for hop in range(3):
            x_arrival(s, hop).wait_recv()
        y_copy(s).start()

    def tick_y(s):
        y_arrival(s).wait_recv()

    def halo_copies(n, base):
        return (
            remote(n.at[pl.ds(OWN + ROWS - 48, 48)], n.at[pl.ds(0, 48)], hs.at[base], hr.at[base], after),
            remote(n.at[pl.ds(OWN, 32)], n.at[pl.ds(OWN + ROWS, 32)], hs.at[base + 1], hr.at[base + 1], before),
        )

    id_copies = (
        remote(ids, ids_prev, hs.at[4], hr.at[4], after),
        remote(ids, ids_next, hs.at[5], hr.at[5], before),
    )

    def normalise(h, n, r0, rows):
        scale = lax.rsqrt(jnp.mean(h * h, axis=1, keepdims=True) + 1e-06)
        n[pl.ds(OWN + r0, rows), :] = (h * scale * gain[...].astype(F32)).astype(BF16)

    loads[0].wait()
    loads[1].wait()

    def first_norm(i, _):
        r0 = pl.multiple_of(i * 48, 48)
        h = st[pl.ds(r0, 48), :].astype(F32) + cd[pl.ds(r0, 48), :].astype(F32)
        normalise(h, n1, r0, 48)
        return 0

    lax.fori_loop(0, ROWS // 48, first_norm, 0)
    loads[2].wait()
    loads[3].wait()

    pl.semaphore_wait(barrier, len(partners))
    for s in range(PARTS):
        z_copy(s).start()
    first_halo = halo_copies(n1, 0)
    for copy in first_halo + id_copies:
        copy.start()

    for p in range(4):
        v[:, 256 * p + 128 : 256 * p + 256] = jnp.ones((EXT, 128), BF16)

    low = lax.broadcasted_iota(jnp.int32, (1, 128), 1) < 64

    def queries(n, w, pair):
        r = jnp.dot(n[OWN : OWN + ROWS, :], w[0], preferred_element_type=F32) * 0.125
        zero = jnp.zeros((), BF16)
        for j in range(2):
            c = 128 * (pair + j)
            part_q = r[:, 128 * j : 128 * j + 128].astype(BF16)
            qa[:, c : c + 128] = jnp.where(low, part_q, zero)
            qb[:, c : c + 128] = jnp.where(low, zero, part_q)

    def keys(n, w, pair, r0, rows):
        r = jnp.dot(n[r0 : r0 + rows, :], w[1], preferred_element_type=F32)
        k[r0 : r0 + rows, 128 * pair : 128 * pair + 256] = r.astype(BF16)

    def values(n, w, pair, r0, rows):
        r = jnp.dot(n[r0 : r0 + rows, :], w[2], preferred_element_type=F32).astype(BF16)
        for j in range(2):
            c = 256 * (pair + j)
            v[r0 : r0 + rows, c : c + 128] = r[:, 128 * j : 128 * j + 128]

    def build_bias():
        lane = lax.broadcasted_iota(jnp.int32, (8, LANES), 1)
        ext = jnp.where(
            lane < OWN,
            jnp.where(seq == 0, -1.0, pltpu.roll(ids_prev[...], LANES - (ROWS - 48), 1)),
            jnp.where(
                lane < OWN + ROWS,
                pltpu.roll(ids[...], OWN, 1),
                jnp.where(seq == 127, -2.0, pltpu.roll(ids_next[...], OWN + ROWS, 1)),
            ),
        )
        row = lax.broadcasted_iota(jnp.int32, (TILE, KEYS), 0)
        col = lax.broadcasted_iota(jnp.int32, (TILE, KEYS), 1)
        first = jnp.where(row < BLOCK, 0, BLOCK)
        window = (col >= first) & (col < first + 4 * BLOCK)
        for t in range(TILES):
            moved = ext if t == 0 else pltpu.roll(ext, LANES - TILE * t, 1)
            key_ids = jnp.broadcast_to(moved[0:1, :KEYS], (TILE, KEYS))
            query_ids = jnp.sum(jnp.where(col == row + OWN, key_ids, 0.0), axis=1, keepdims=True)
            bias[TILE * t : TILE * t + TILE, :] = jnp.where(window & (query_ids == key_ids), 0.0, -1e30)

    def attend(r0, pairs):
        b = bias[pl.ds(r0, TILE), :]
        b2 = jnp.concatenate([b, b], axis=0)
        for p in pairs:
            c = 128 * p
            q2 = jnp.concatenate([qa[pl.ds(r0, TILE), c : c + 128], qb[pl.ds(r0, TILE), c : c + 128]], axis=0)
            scores = lax.dot_general(
                q2, k[pl.ds(r0, KEYS), c : c + 128], (((1,), (1,)), ((), ())), preferred_element_type=F32
            )
            scores = scores + b2
            e = jnp.exp(scores - jnp.max(scores, axis=1, keepdims=True)).astype(BF16)
            o = jnp.dot(e, v[pl.ds(r0, KEYS), 2 * c : 2 * c + 256], preferred_element_type=F32)
            num = jnp.where(low, o[:TILE, :128], o[TILE:, :128])
            den = jnp.where(low, o[:TILE, 128:], o[TILE:, 128:])
            att[pl.ds(r0, TILE), c : c + 128] = (num / den).astype(BF16)

    def attend_some(tiles, pairs):
        start, stop = tiles

        def body(i, _):
            for j in range(2):
                attend(pl.multiple_of((start + 2 * i + j) * TILE, TILE), pairs)
            return 0

        lax.fori_loop(0, (stop - start) // 2, body, 0)

    queries(n1, wq, 0)
    for copy in first_halo + id_copies:
        copy.wait_recv()
    keys(n1, wq, 0, 0, EXT)
    values(n1, wq, 0, 0, EXT)
    tick_z(0)
    build_bias()
    attend_some((0, 4), (0, 1))
    tick_z(1)
    attend_some((4, 10), (0, 1))
    tick_z(2)
    tick_x(0)
    for c in range(0, D, 512):
        acc[:, c : c + 512] = jnp.dot(att[:, :256], wo[:, c : c + 512], preferred_element_type=F32)
    tick_z(3)
    tick_x(1)
    tick_z(4)
    tick_x(2)
    tick_y(0)
    tick_z(5)
    tick_x(3)
    tick_y(1)
    queries(n1, fq, 2)
    tick_z(6)
    tick_x(4)
    tick_y(2)
    tick_z(7)
    tick_x(5)
    tick_y(3)
    keys(n1, fq, 2, 0, EXT)
    tick_x(6)
    tick_y(4)
    tick_x(7)
    tick_y(5)
    values(n1, fq, 2, 0, EXT)
    attend_some((0, TILES), (2, 3))
    tick_y(6)
    tick_y(7)

    def pv_copy(r):
        rows = pl.ds(CHUNK * r, CHUNK)
        return remote(pv_out.at[rows], pv_in.at[rows], ds.at[r], dr.at[r], twin)

    for r in BOUNDARY_FIRST:
        rows = slice(CHUNK * r, CHUNK * r + CHUNK)
        total = acc[rows, :] + jnp.dot(att[rows, 256:512], fo[...], preferred_element_type=F32)
        acc[rows, :] = total
        pv_out[rows, :] = total.astype(BF16)
        pv_copy(r).start()

    second_halo = halo_copies(n2, 2)
    for r in BOUNDARY_FIRST:
        pv_copy(r).wait_recv()
        for r0 in range(CHUNK * r, CHUNK * r + CHUNK, 48):
            rows = slice(r0, r0 + 48)
            x_new = st[rows, :].astype(F32) + 0.5 * (acc[rows, :] + pv_in[rows, :].astype(F32))
            x1[rows, :] = x_new
            h = x_new + cd[rows, :].astype(F32) + 0.5 * tvec[...].astype(F32)
            normalise(h, n2, r0, 48)
        if r == 0:
            second_halo[1].start()
        if r == CHUNKS - 1:
            second_halo[0].start()

    for w, pair in ((wq, 0), (fq, 2)):
        queries(n2, w, pair)
        keys(n2, w, pair, OWN, ROWS)
        values(n2, w, pair, OWN, ROWS)
    attend_some((1, 9), range(4))
    for copy in second_halo:
        copy.wait_recv()
    for w, pair in ((wq, 0), (fq, 2)):
        for r0, rows in ((0, OWN), (OWN + ROWS, 32)):
            keys(n2, w, pair, r0, rows)
            values(n2, w, pair, r0, rows)
    attend(0, range(4))
    attend((TILES - 1) * TILE, range(4))

    my_cols = pl.ds(pl.multiple_of(512 * zh + 256 * core, 256), 256)
    twin_cols = pl.ds(pl.multiple_of(512 * zh + 256 * (1 - core), 256), 256)

    def terms(cols):
        return jnp.dot(att[:, :256], wo[:, cols], preferred_element_type=F32) + jnp.dot(
            att[:, 256:512], fo[:, cols], preferred_element_type=F32
        )

    fin_out[...] = terms(twin_cols).astype(BF16)
    fin_copy = remote(fin_out, fin_in, ds.at[CHUNKS], dr.at[CHUNKS], twin)
    fin_copy.start()
    acc[:, 0:256] = x1[:, my_cols] + 0.5 * terms(my_cols)
    fin_copy.wait_recv()
    out[...] = (acc[:, 0:256] + 0.5 * fin_in[...].astype(F32)).astype(BF16)

    for s in range(PARTS):
        z_copy(s).wait_send()
        for hop in range(3):
            x_copy(s, hop).wait_send()
        y_copy(s).wait_send()
    for copy in first_halo + id_copies + second_halo:
        copy.wait_send()
    for r in range(CHUNKS):
        pv_copy(r).wait_send()
    fin_copy.wait_send()


def shards(state, condition, time_vector, norm_gain, w_qkv, w_out, utterance_ids):
    ids = jnp.broadcast_to(jnp.pad(utterance_ids.astype(F32), (0, LANES - ROWS)), (8, LANES))
    any_spec = pl.BlockSpec(memory_space=pl.ANY)
    vmem = pl.BlockSpec(memory_space=pltpu.VMEM)
    dma = pltpu.SemaphoreType.DMA
    return pl.pallas_call(
        kernel,
        out_shape=jax.ShapeDtypeStruct((ROWS, 256), BF16),
        in_specs=[any_spec] * 4 + [vmem] * 3,
        out_specs=vmem,
        scratch_shapes=[
            pltpu.VMEM((ROWS, D), BF16),
            pltpu.VMEM((ROWS, D), BF16),
            pltpu.VMEM((3, D, 256), BF16),
            pltpu.VMEM((256, D), BF16),
            pltpu.VMEM((3, D, 256), BF16),
            pltpu.VMEM((256, D), BF16),
            pltpu.VMEM((EXT, D), BF16),
            pltpu.VMEM((EXT, D), BF16),
            pltpu.VMEM((8, LANES), F32),
            pltpu.VMEM((8, LANES), F32),
            pltpu.VMEM((ROWS, KEYS), F32),
            pltpu.VMEM((ROWS, 512), BF16),
            pltpu.VMEM((ROWS, 512), BF16),
            pltpu.VMEM((EXT, 512), BF16),
            pltpu.VMEM((EXT, 1024), BF16),
            pltpu.VMEM((ROWS, 512), BF16),
            pltpu.VMEM((ROWS, D), F32),
            pltpu.VMEM((ROWS, D), BF16),
            pltpu.VMEM((ROWS, D), BF16),
            pltpu.VMEM((ROWS, D), F32),
            pltpu.VMEM((ROWS, 256), BF16),
            pltpu.VMEM((ROWS, 256), BF16),
            dma((4,)),
            dma((PARTS,)),
            dma((PARTS,)),
            dma((3 * PARTS,)),
            dma((3 * PARTS,)),
            dma((PARTS,)),
            dma((PARTS,)),
            dma((6,)),
            dma((6,)),
            dma((CHUNKS + 1,)),
            dma((CHUNKS + 1,)),
        ],
        compiler_params=pltpu.CompilerParams(
            collective_id=0, has_side_effects=True, vmem_limit_bytes=48 << 20
        ),
        cost_estimate=pl.CostEstimate(flops=4_500_000_000, bytes_accessed=4_500_000, transcendentals=1_500_000),
        name="decoder",
    )(state, condition, w_qkv, w_out, time_vector.reshape(1, D), norm_gain.reshape(1, D), ids)


def solution(mesh):
    in_specs = (
        P("seq", None),
        P("seq", None),
        P(),
        P(),
        P(None, None, "mp"),
        P("mp", None),
        P("seq"),
    )
    out_specs = P("seq", "mp")
    return jax.shard_map(shards, mesh=mesh, in_specs=in_specs, out_specs=out_specs, check_vma=False)
```

time: 269 us -> 80.4 us (0.30)
  the two profiles are of different devices: /device:TPU:1 before, /device:TPU:9 now
where the time goes in v1:
time: 80.4 us; the launch traced here: 80.1 us
  Pallas kernels  72.5 us (90%)
  local copies, waits for them, and re-layouts  6.92 us (9%)
    pallas_call x1, Pallas kernels, shards(): pl.pallas_call(kernel, out_shape=jax.ShapeDtypeStruct((ROWS, 256), BF16),...  72.5 us
    unnamed x9, local copies, waits for them, and re-layouts  5.54 us

profile of v1, /device:TPU:9, one launch (start us, length us, event | category | flops | bytes accessed | tf_op | source)
XLA Modules:
  0.0 80.1 jit_solution(18028203261127620013)
XLA Ops:
  0.0 0.7 convert_element_type.5
  0.7 0.7 reshape.6.tvec
  1.4 0.7 reshape.7.gain
  2.1 0.0 copy-start
  2.1 1.4 %copy-done = bf16[3,1024,256]{2,1,0:T(8,128)(2,1)S(1)} copy-done((bf16[3,1024,256]{2,1,0:T(8,128)(2,1)S(1)}, bf16[3,1024,256]{2,1,0:T(8,128)(2,1)}, u32[]{:S(2)}) %copy-start) | copy-done | bytes 1572888
  3.5 0.0 copy-start.1
  3.5 1.2 %copy-done.1 = bf16[480,1024]{1,0:T(8,128)(2,1)S(1)} copy-done((bf16[480,1024]{1,0:T(8,128)(2,1)S(1)}, bf16[480,1024]{1,0:T(8,128)(2,1)}, u32[]{:S(2)}) %copy-start.1) | copy-done | bytes 983064
  4.7 0.0 copy-start.2
  4.7 1.2 %copy-done.2 = bf16[480,1024]{1,0:T(8,128)(2,1)S(1)} copy-done((bf16[480,1024]{1,0:T(8,128)(2,1)S(1)}, bf16[480,1024]{1,0:T(8,128)(2,1)}, u32[]{:S(2)}) %copy-start.2) | copy-done | bytes 983064
  5.9 0.0 copy-start.3
  5.9 1.0 %copy-done.3 = bf16[256,1024]{1,0:T(8,128)(2,1)S(1)} copy-done((bf16[256,1024]{1,0:T(8,128)(2,1)S(1)}, bf16[256,1024]{1,0:T(8,128)(2,1)}, u32[]{:S(2)}) %copy-start.3) | copy-done | bytes 524312
  6.9 72.5 %decoder.1 = bf16[480,256]{1,0:T(8,128)(2,1)S(1)} custom-call(bf16[480,1024]{1,0:T(8,128)(2,1)S(1)} %copy-done.1, bf16[480,1024]{1,0:T(8,128)(2,1)S(1)} %copy-done.2, bf16[3,1024,256]{2,1,0:T(8,128)(2,1)S(1)} %copy-done, bf16[256,1024]{1,0:T(8,128)(2,1)S(1)} %copy-done.3, bf16[1,1024]{1,0:T(2,128)(2,1)S(1)} %reshape.6.tvec, ...), custom_call_target="tpu_custom_call" | custom-call | flops 4499999744 | bytes 4500000 | tf_op jit(solution)/shard_map/decoder/pallas_call | solution.py:323
  79.4 0.7 copy.9
  (2 shorter events, 0.0 us)
Async XLA Ops:
  2.1 1.4 %copy-start = (bf16[3,1024,256]{2,1,0:T(8,128)(2,1)S(1)}, bf16[3,1024,256]{2,1,0:T(8,128)(2,1)}, u32[]{:S(2)}) copy-start(bf16[3,1024,256]{2,1,0:T(8,128)(2,1)} %wqkv_h.1) | copy-start | bytes 4718596
  3.5 1.2 %copy-start.1 = (bf16[480,1024]{1,0:T(8,128)(2,1)S(1)}, bf16[480,1024]{1,0:T(8,128)(2,1)}, u32[]{:S(2)}) copy-start(bf16[480,1024]{1,0:T(8,128)(2,1)} %state_h.1) | copy-start | bytes 2949124
  4.7 1.2 %copy-start.2 = (bf16[480,1024]{1,0:T(8,128)(2,1)S(1)}, bf16[480,1024]{1,0:T(8,128)(2,1)}, u32[]{:S(2)}) copy-start(bf16[480,1024]{1,0:T(8,128)(2,1)} %cond_h.1) | copy-start | bytes 2949124
  5.9 1.0 %copy-start.3 = (bf16[256,1024]{1,0:T(8,128)(2,1)S(1)}, bf16[256,1024]{1,0:T(8,128)(2,1)}, u32[]{:S(2)}) copy-start(bf16[256,1024]{1,0:T(8,128)(2,1)} %wout_h.1) | copy-start | bytes 1572868

commit v2 on v1

v2 whole, which is shorter than its diff:
```python
import jax
import jax.numpy as jnp
from jax import lax
from jax.experimental import pallas as pl
from jax.experimental.pallas import tpu as pltpu
from jax.sharding import PartitionSpec as P

MESH = pl.DeviceIdType.MESH
BF16 = jnp.bfloat16
F32 = jnp.float32

D = 1024
BLOCK = 24
ROWS = 480
EXT = 560
OWN = 48
TILE = 48
KEYS = 128
TILES = ROWS // TILE
LANES = 640
CHUNK = 96
CHUNKS = ROWS // CHUNK
BOUNDARY_FIRST = (0, CHUNKS - 1) + tuple(range(1, CHUNKS - 1))
PARTS = 8


def kernel(
    state_h, cond_h, wqkv_h, wout_h, tvec_h, gain_h, ids_h, out,
    st, cd, wq, wo, fq, fo, tvec, gain, ids, n1, n2, h1, h2, ids_prev, ids_next, bias, qa, qb, k, v, att, acc,
    pv_out, pv_in, x1, fin_out, fin_in,
    load_sem, zs, zf, zr, xs, xr, ys, yr, hs, hr, ds, dr,
):
    seq = lax.axis_index("seq")
    mp = lax.axis_index("mp")
    x = seq % 4
    y = seq // 16
    odd = y % 2
    zh = mp // 2
    core = mp % 2
    colour = (x + 2 * odd) % 4

    zl = (seq // 4) % 4
    up = (jnp.where(zl == 3, seq - 12, seq + 4), jnp.where(zl == 3, 1 - zh, zh) * 2 + core)
    down = (jnp.where(zl == 0, seq + 12, seq - 4), jnp.where(zl == 0, 1 - zh, zh) * 2 + core)
    outer = (zl == 0) | (zl == 3)
    across = [jnp.where(zl == 3, a, b) for a, b in zip(up, down)]
    inward = [jnp.where(zl == 3, b, a) for a, b in zip(up, down)]
    at_x = [(seq - x + (x + hop) % 4, mp) for hop in (1, 3)]
    at_y = [((seq + 16 * hop) % 128, mp) for hop in (1, 7)]
    before = ((seq + 127) % 128, mp)
    after = ((seq + 1) % 128, mp)
    twin = (seq, zh * 2 + 1 - core)

    barrier = pltpu.get_barrier_semaphore()
    partners = [up, down] + at_x + at_y + [twin]
    for device in partners:
        pl.semaphore_signal(barrier, inc=1, device_id=device, device_id_type=MESH)

    has_before = seq > 0
    has_after = seq < 127

    @pl.when(has_before)
    def _():
        pl.semaphore_signal(barrier, inc=1, device_id=before, device_id_type=MESH)

    @pl.when(has_after)
    def _():
        pl.semaphore_signal(barrier, inc=1, device_id=after, device_id_type=MESH)

    loads = [
        pltpu.make_async_copy(src, dst, load_sem.at[i])
        for i, (src, dst) in enumerate(
            (
                (gain_h, gain),
                (state_h, st),
                (cond_h, cd),
                (ids_h, ids),
                (wqkv_h, wq),
                (wout_h, wo),
                (tvec_h, tvec),
            )
        )
    ]
    for load in loads:
        load.start()

    def remote(src, dst, send, recv, device):
        return pltpu.make_async_remote_copy(
            src_ref=src, dst_ref=dst, send_sem=send, recv_sem=recv, device_id=device, device_id_type=MESH
        )

    def piece(pair, s, which, half=None):
        size, ref = (128, pair[0].at[s // 2]) if s < 6 else (32, pair[1])
        first = 4 * size * (s % 2) + size * which
        if half is not None:
            size = size // 2
            first = first + size * half
        return ref.at[pl.ds(pl.multiple_of(first, 16), size)]

    mine, foreign = (wqkv_h, wout_h), (fq, fo)

    def z_copy(s):
        return remote(piece(mine, s, colour), piece(foreign, s, colour), zs.at[s], zr.at[s], across)

    def z_forward(s):
        return remote(piece(foreign, s, colour), piece(foreign, s, colour), zf.at[s], zr.at[s], inward)

    def x_copy(s, j, which):
        i = 2 * s + j
        return remote(piece(foreign, s, which), piece(foreign, s, which), xs.at[i], xr.at[i], at_x[j])

    def y_copy(s, j, which):
        i = 2 * s + j
        return remote(piece(foreign, s, which, j), piece(foreign, s, which, j), ys.at[i], yr.at[i], at_y[j])

    def tick(s):
        z_copy(s).wait_recv()

        @pl.when(outer)
        def _():
            z_forward(s).start()

        for j in range(2):
            x_copy(s, j, colour).start()
            y_copy(s, j, colour).start()

    def complete(s):
        for j in range(2):
            x_copy(s, j, (colour + 3 - 2 * j) % 4).wait_recv()
            y_copy(s, j, (colour + 2) % 4).wait_recv()

    def halo_copies(n, h, base):
        return (
            remote(n.at[pl.ds(ROWS - 48, 48)], h.at[pl.ds(0, 48)], hs.at[base], hr.at[base], after),
            remote(n.at[pl.ds(0, 32)], h.at[pl.ds(48, 32)], hs.at[base + 1], hr.at[base + 1], before),
        )

    id_copies = (
        remote(ids, ids_prev, hs.at[4], hr.at[4], after),
        remote(ids, ids_next, hs.at[5], hr.at[5], before),
    )

    def send_after(copies):
        @pl.when(has_after)
        def _():
            for copy in copies:
                copy.start()

    def send_before(copies):
        @pl.when(has_before)
        def _():
            for copy in copies:
                copy.start()

    def halo_arrived(copies):
        @pl.when(has_before)
        def _():
            for copy in copies[::2]:
                copy.wait_recv()

        @pl.when(has_after)
        def _():
            for copy in copies[1::2]:
                copy.wait_recv()

    def halo_left(copies):
        @pl.when(has_after)
        def _():
            for copy in copies[::2]:
                copy.wait_send()

        @pl.when(has_before)
        def _():
            for copy in copies[1::2]:
                copy.wait_send()

    def normalise(h, n, r0, rows):
        scale = lax.rsqrt(jnp.mean(h * h, axis=1, keepdims=True) + 1e-06)
        n[pl.ds(r0, rows), :] = (h * scale * gain[...].reshape(1, D).astype(F32)).astype(BF16)

    pl.semaphore_wait(barrier, len(partners) + jnp.where(has_before & has_after, 2, 1))

    @pl.when(outer)
    def _():
        for s in range(PARTS):
            z_copy(s).start()

    for load in loads[:4]:
        load.wait()

    def first_norm(i, _):
        r0 = pl.multiple_of(i * 48, 48)
        h = st[pl.ds(r0, 48), :].astype(F32) + cd[pl.ds(r0, 48), :].astype(F32)
        normalise(h, n1, r0, 48)
        return 0

    lax.fori_loop(0, ROWS // 48, first_norm, 0)
    first_halo = halo_copies(n1, h1, 0)
    send_after((first_halo[0], id_copies[0]))
    send_before((first_halo[1], id_copies[1]))

    @pl.when(seq == 0)
    def _():
        for h in (h1, h2):
            h[0:48, :] = jnp.zeros((48, D), BF16)

    @pl.when(seq == 127)
    def _():
        for h in (h1, h2):
            h[48:80, :] = jnp.zeros((32, D), BF16)

    for load in loads[4:]:
        load.wait()

    for p in range(4):
        v[:, 256 * p + 128 : 256 * p + 256] = jnp.ones((EXT, 128), BF16)

    low = lax.broadcasted_iota(jnp.int32, (1, 128), 1) < 64

    def queries(n, w, pair):
        r = jnp.dot(n[...], w[0], preferred_element_type=F32) * 0.125
        zero = jnp.zeros((), BF16)
        for j in range(2):
            c = 128 * (pair + j)
            part_q = r[:, 128 * j : 128 * j + 128].astype(BF16)
            qa[:, c : c + 128] = jnp.where(low, part_q, zero)
            qb[:, c : c + 128] = jnp.where(low, zero, part_q)

    def spans(halo):
        return ((0, 0, 48), (48, OWN + ROWS, 32)) if halo else ((0, OWN, ROWS),)

    def keys(n, w, pair, halo=False):
        r = jnp.dot(n[...], w[1], preferred_element_type=F32).astype(BF16)
        for r0, to, rows in spans(halo):
            k[to : to + rows, 128 * pair : 128 * pair + 256] = r[r0 : r0 + rows]

    def values(n, w, pair, halo=False):
        r = jnp.dot(n[...], w[2], preferred_element_type=F32).astype(BF16)
        for r0, to, rows in spans(halo):
            for j in range(2):
                c = 256 * (pair + j)
                v[to : to + rows, c : c + 128] = r[r0 : r0 + rows, 128 * j : 128 * j + 128]

    def build_bias():
        lane = lax.broadcasted_iota(jnp.int32, (8, LANES), 1)

        def wide(ref):
            flat = ref[...].astype(F32).reshape(1, ROWS)
            flat = jnp.concatenate([flat, jnp.zeros((1, LANES - ROWS), F32)], axis=1)
            return jnp.broadcast_to(flat, (8, LANES))

        ext = jnp.where(
            lane < OWN,
            jnp.where(seq == 0, -1.0, pltpu.roll(wide(ids_prev), LANES - (ROWS - 48), 1)),
            jnp.where(
                lane < OWN + ROWS,
                pltpu.roll(wide(ids), OWN, 1),
                jnp.where(seq == 127, -2.0, pltpu.roll(wide(ids_next), OWN + ROWS, 1)),
            ),
        )
        row = lax.broadcasted_iota(jnp.int32, (TILE, KEYS), 0)
        col = lax.broadcasted_iota(jnp.int32, (TILE, KEYS), 1)
        first = jnp.where(row < BLOCK, 0, BLOCK)
        window = (col >= first) & (col < first + 4 * BLOCK)
        for t in range(TILES):
            moved = ext if t == 0 else pltpu.roll(ext, LANES - TILE * t, 1)
            key_ids = jnp.broadcast_to(moved[0:1, :KEYS], (TILE, KEYS))
            query_ids = jnp.sum(jnp.where(col == row + OWN, key_ids, 0.0), axis=1, keepdims=True)
            bias[TILE * t : TILE * t + TILE, :] = jnp.where(window & (query_ids == key_ids), 0.0, -1e30)

    def attend(starts, pairs):
        scores = []
        for r0 in starts:
            b = bias[pl.ds(r0, TILE), :]
            b2 = jnp.concatenate([b, b], axis=0)
            for p in pairs:
                c = 128 * p
                q2 = jnp.concatenate([qa[pl.ds(r0, TILE), c : c + 128], qb[pl.ds(r0, TILE), c : c + 128]], axis=0)
                scores.append(
                    lax.dot_general(
                        q2, k[pl.ds(r0, KEYS), c : c + 128], (((1,), (1,)), ((), ())), preferred_element_type=F32
                    )
                    + b2
                )
        tops = [jnp.max(score, axis=1, keepdims=True) for score in scores]
        exps = [jnp.exp(score - top).astype(BF16) for score, top in zip(scores, tops)]
        where = [(r0, 128 * p) for r0 in starts for p in pairs]
        sums = [
            jnp.dot(e, v[pl.ds(r0, KEYS), 2 * c : 2 * c + 256], preferred_element_type=F32)
            for e, (r0, c) in zip(exps, where)
        ]
        for o, (r0, c) in zip(sums, where):
            num = jnp.where(low, o[:TILE, :128], o[TILE:, :128])
            den = jnp.where(low, o[:TILE, 128:], o[TILE:, 128:])
            att[pl.ds(r0, TILE), c : c + 128] = (num / den).astype(BF16)

    def attend_some(start, count, groups, pairs):
        def body(i, _):
            attend([pl.multiple_of((start + count * i + j) * TILE, TILE) for j in range(count)], pairs)
            return 0

        lax.fori_loop(0, groups, body, 0)

    queries(n1, wq, 0)
    tick(0)
    keys(n1, wq, 0)
    tick(1)
    values(n1, wq, 0)
    tick(2)
    tick(3)
    tick(4)
    halo_arrived(first_halo + id_copies)
    keys(h1, wq, 0, True)
    values(h1, wq, 0, True)
    build_bias()
    tick(5)
    attend_some(0, 5, 1, (0, 1))
    tick(6)
    attend_some(5, 5, 1, (0, 1))
    tick(7)
    complete(0)
    complete(1)
    queries(n1, fq, 2)
    for c in range(0, D, 512):
        acc[:, c : c + 512] = jnp.dot(att[:, :256], wo[:, c : c + 512], preferred_element_type=F32)
    complete(2)
    complete(3)
    keys(n1, fq, 2)
    keys(h1, fq, 2, True)
    complete(4)
    complete(5)
    values(n1, fq, 2)
    values(h1, fq, 2, True)
    attend_some(0, 5, 2, (2, 3))
    complete(6)
    complete(7)

    def pv_copy(r):
        rows = pl.ds(CHUNK * r, CHUNK)
        return remote(pv_out.at[rows], pv_in.at[rows], ds.at[r], dr.at[r], twin)

    for r in BOUNDARY_FIRST:
        rows = slice(CHUNK * r, CHUNK * r + CHUNK)
        total = acc[rows, :] + jnp.dot(att[rows, 256:512], fo[...], preferred_element_type=F32)
        acc[rows, :] = total
        pv_out[rows, :] = total.astype(BF16)
        pv_copy(r).start()

    second_halo = halo_copies(n2, h2, 2)
    for r in BOUNDARY_FIRST:
        pv_copy(r).wait_recv()
        for r0 in range(CHUNK * r, CHUNK * r + CHUNK, 48):
            rows = slice(r0, r0 + 48)
            x_new = st[rows, :].astype(F32) + 0.5 * (acc[rows, :] + pv_in[rows, :].astype(F32))
            x1[rows, :] = x_new
            h = x_new + cd[rows, :].astype(F32) + 0.5 * tvec[...].reshape(1, D).astype(F32)
            normalise(h, n2, r0, 48)
        if r == 0:
            send_before(second_halo[1:])
        if r == CHUNKS - 1:
            send_after(second_halo[:1])

    for w, pair in ((wq, 0), (fq, 2)):
        queries(n2, w, pair)
        keys(n2, w, pair)
        values(n2, w, pair)
    my_cols = pl.ds(pl.multiple_of(512 * zh + 256 * core, 256), 256)
    twin_cols = pl.ds(pl.multiple_of(512 * zh + 256 * (1 - core), 256), 256)

    def terms(r0, rows, cols):
        a = att[r0 : r0 + rows, :]
        return jnp.dot(a[:, :256], wo[:, cols], preferred_element_type=F32) + jnp.dot(
            a[:, 256:512], fo[:, cols], preferred_element_type=F32
        )

    INNER, FIRST, LAST = (TILE, ROWS - 2 * TILE), (0, TILE), (ROWS - TILE, TILE)

    def fin_copy(i, r0, rows):
        span = pl.ds(r0, rows)
        return remote(fin_out.at[span], fin_in.at[span], ds.at[CHUNKS + i], dr.at[CHUNKS + i], twin)

    def send_terms(i, r0, rows):
        fin_out[r0 : r0 + rows, :] = terms(r0, rows, twin_cols).astype(BF16)
        fin_copy(i, r0, rows).start()

    def finish(i, r0, rows):
        fin_copy(i, r0, rows).wait_recv()
        span = slice(r0, r0 + rows)
        out[span, :] = (acc[span, 0:256] + 0.5 * fin_in[span, :].astype(F32)).astype(BF16)

    def own_terms(r0, rows):
        acc[r0 : r0 + rows, 0:256] = x1[r0 : r0 + rows, my_cols] + 0.5 * terms(r0, rows, my_cols)

    attend_some(1, 4, 2, range(4))
    send_terms(0, *INNER)
    own_terms(*INNER)
    halo_arrived(second_halo)
    for w, pair in ((wq, 0), (fq, 2)):
        keys(h2, w, pair, True)
        values(h2, w, pair, True)
    attend((0, (TILES - 1) * TILE), range(4))
    send_terms(1, *FIRST)
    send_terms(2, *LAST)
    own_terms(*FIRST)
    own_terms(*LAST)
    for i, span in enumerate((INNER, FIRST, LAST)):
        finish(i, *span)

    for s in range(PARTS):


        @pl.when(outer)
        def _():
            z_copy(s).wait_send()
            z_forward(s).wait_send()

        for j in range(2):
            x_copy(s, j, colour).wait_send()
            y_copy(s, j, colour).wait_send()
    halo_left(first_halo + id_copies + second_halo)
    for r in range(CHUNKS):
        pv_copy(r).wait_send()
    for i, span in enumerate((INNER, FIRST, LAST)):
        fin_copy(i, *span).wait_send()


def shards(state, condition, time_vector, norm_gain, w_qkv, w_out, utterance_ids):
    any_spec = pl.BlockSpec(memory_space=pl.ANY)
    vmem = pl.BlockSpec(memory_space=pltpu.VMEM)
    dma = pltpu.SemaphoreType.DMA
    return pl.pallas_call(
        kernel,
        out_shape=jax.ShapeDtypeStruct((ROWS, 256), BF16),
        in_specs=[any_spec] * 7,
        out_specs=vmem,
        scratch_shapes=[
            pltpu.VMEM((ROWS, D), BF16),
            pltpu.VMEM((ROWS, D), BF16),
            pltpu.VMEM((3, D, 256), BF16),
            pltpu.VMEM((256, D), BF16),
            pltpu.VMEM((3, D, 256), BF16),
            pltpu.VMEM((256, D), BF16),
            pltpu.VMEM((D,), BF16),
            pltpu.VMEM((D,), BF16),
            pltpu.VMEM((ROWS,), jnp.int32),
            pltpu.VMEM((ROWS, D), BF16),
            pltpu.VMEM((ROWS, D), BF16),
            pltpu.VMEM((80, D), BF16),
            pltpu.VMEM((80, D), BF16),
            pltpu.VMEM((ROWS,), jnp.int32),
            pltpu.VMEM((ROWS,), jnp.int32),
            pltpu.VMEM((ROWS, KEYS), F32),
            pltpu.VMEM((ROWS, 512), BF16),
            pltpu.VMEM((ROWS, 512), BF16),
            pltpu.VMEM((EXT, 512), BF16),
            pltpu.VMEM((EXT, 1024), BF16),
            pltpu.VMEM((ROWS, 512), BF16),
            pltpu.VMEM((ROWS, D), F32),
            pltpu.VMEM((ROWS, D), BF16),
            pltpu.VMEM((ROWS, D), BF16),
            pltpu.VMEM((ROWS, D), F32),
            pltpu.VMEM((ROWS, 256), BF16),
            pltpu.VMEM((ROWS, 256), BF16),
            dma((7,)),
            dma((PARTS,)),
            dma((PARTS,)),
            dma((PARTS,)),
            dma((2 * PARTS,)),
            dma((2 * PARTS,)),
            dma((2 * PARTS,)),
            dma((2 * PARTS,)),
            dma((6,)),
            dma((6,)),
            dma((CHUNKS + 3,)),
            dma((CHUNKS + 3,)),
        ],
        compiler_params=pltpu.CompilerParams(
            collective_id=0, has_side_effects=True, vmem_limit_bytes=62 << 20
        ),
        cost_estimate=pl.CostEstimate(flops=4_500_000_000, bytes_accessed=4_500_000, transcendentals=1_500_000),
        name="decoder",
    )(state, condition, w_qkv, w_out, time_vector, norm_gain, utterance_ids)


def solution(mesh):
    in_specs = (
        P("seq", None),
        P("seq", None),
        P(),
        P(),
        P(None, None, "mp"),
        P("mp", None),
        P("seq"),
    )
    out_specs = P("seq", "mp")
    return jax.shard_map(shards, mesh=mesh, in_specs=in_specs, out_specs=out_specs, check_vma=False)
```

time: 80.4 us -> 46.5 us (0.58)
  the two profiles are of different devices: /device:TPU:9 before, /device:TPU:49 now
where the time goes in v2:
time: 46.5 us; the launch traced here: 46.4 us
  Pallas kernels  44.7 us (96%)
  local copies, waits for them, and re-layouts  1.65 us (4%)
    pallas_call x1, Pallas kernels, shards(): pl.pallas_call(kernel, out_shape=jax.ShapeDtypeStruct((ROWS, 256), BF16),...  44.7 us
    unnamed x1, local copies, waits for them, and re-layouts  1.65 us

profile of v2, /device:TPU:49, one launch (start us, length us, event | category | flops | bytes accessed | tf_op | source)
XLA Modules:
  0.0 46.4 jit_solution(3579239210593729488)
XLA Ops:
  0.0 44.7 %decoder.1 = bf16[480,256]{1,0:T(8,128)(2,1)} custom-call(bf16[480,1024]{1,0:T(8,128)(2,1)} %state_h.1, bf16[480,1024]{1,0:T(8,128)(2,1)} %cond_h.1, bf16[3,1024,256]{2,1,0:T(8,128)(2,1)} %wqkv_h.1, bf16[256,1024]{1,0:T(8,128)(2,1)} %wout_h.1, bf16[1024]{0:T(1024)(128)(2,1)} %tvec_h.1, bf16[1024]{0:T(1024)(128)(2,1)} %gain_h.1, s32[480]{0:T(512)} %ids_h.1), custom_call_target="tpu_custom_call" | custom-call | flops 4499999744 | bytes 4500000 | tf_op jit(solution)/shard_map/decoder/pallas_call | solution.py:431
  44.7 1.7 %copy.9 = bf16[480,256]{1,0:T(8,128)(2,1)} copy(bf16[480,256]{1,0:T(8,128)(2,1)} %decoder.1) | data formatting | bytes 491520

commit v3 on v2

--- a/solution.py
+++ b/solution.py
@@ -18,16 +18,14 @@
 KEYS = 128
 TILES = ROWS // TILE
 LANES = 640
-CHUNK = 96
-CHUNKS = ROWS // CHUNK
-BOUNDARY_FIRST = (0, CHUNKS - 1) + tuple(range(1, CHUNKS - 1))
+CHUNKS = ((ROWS - 48, 48), (0, 48)) + tuple((r, 96) for r in range(48, ROWS - 48, 96))
 PARTS = 8
 
 
 def kernel(
     state_h, cond_h, wqkv_h, wout_h, tvec_h, gain_h, ids_h, out,
     st, cd, wq, wo, fq, fo, tvec, gain, ids, n1, n2, h1, h2, ids_prev, ids_next, bias, qa, qb, k, v, att, acc,
-    pv_out, pv_in, x1, fin_out, fin_in,
+    pv_out, pv_in, x2, fin_out, fin_in,
     load_sem, zs, zf, zr, xs, xr, ys, yr, hs, hr, ds, dr,
 ):
     seq = lax.axis_index("seq")
@@ -335,35 +333,38 @@
     complete(6)
     complete(7)
 
-    def pv_copy(r):
-        rows = pl.ds(CHUNK * r, CHUNK)
-        return remote(pv_out.at[rows], pv_in.at[rows], ds.at[r], dr.at[r], twin)
-
-    for r in BOUNDARY_FIRST:
-        rows = slice(CHUNK * r, CHUNK * r + CHUNK)
-        total = acc[rows, :] + jnp.dot(att[rows, 256:512], fo[...], preferred_element_type=F32)
-        acc[rows, :] = total
-        pv_out[rows, :] = total.astype(BF16)
-        pv_copy(r).start()
+    def pv_copy(i):
+        span = pl.ds(*CHUNKS[i])
+        return remote(pv_out.at[span], pv_in.at[span], ds.at[i], dr.at[i], twin)
+
+    for i, (r0, rows) in enumerate(CHUNKS):
+        span = slice(r0, r0 + rows)
+        total = acc[span, :] + jnp.dot(att[span, 256:512], fo[...], preferred_element_type=F32)
+        acc[span, :] = total
+        pv_out[span, :] = total.astype(BF16)
+        pv_copy(i).start()
 
     second_halo = halo_copies(n2, h2, 2)
-    for r in BOUNDARY_FIRST:
-        pv_copy(r).wait_recv()
-        for r0 in range(CHUNK * r, CHUNK * r + CHUNK, 48):
-            rows = slice(r0, r0 + 48)
-            x_new = st[rows, :].astype(F32) + 0.5 * (acc[rows, :] + pv_in[rows, :].astype(F32))
-            x1[rows, :] = x_new
-            h = x_new + cd[rows, :].astype(F32) + 0.5 * tvec[...].reshape(1, D).astype(F32)
+    for i, (start, rows) in enumerate(CHUNKS):
+        pv_copy(i).wait_recv()
+        for r0 in range(start, start + rows, 48):
+            span = slice(r0, r0 + 48)
+            x_new = st[span, :].astype(F32) + 0.5 * (acc[span, :] + pv_in[span, :].astype(F32))
+            h = x_new + cd[span, :].astype(F32) + 0.5 * tvec[...].reshape(1, D).astype(F32)
             normalise(h, n2, r0, 48)
-        if r == 0:
+        if i == 0:
+            send_after(second_halo[:1])
+        if i == 1:
             send_before(second_halo[1:])
-        if r == CHUNKS - 1:
-            send_after(second_halo[:1])
-
-    for w, pair in ((wq, 0), (fq, 2)):
-        queries(n2, w, pair)
-        keys(n2, w, pair)
-        values(n2, w, pair)
+
+    queries(n2, wq, 0)
+    keys(n2, wq, 0)
+    values(n2, wq, 0)
+    queries(n2, fq, 2)
+    keys(n2, fq, 2)
+    attend([TILE * t for t in range(1, 9)], (0, 1))
+    values(n2, fq, 2)
+
     my_cols = pl.ds(pl.multiple_of(512 * zh + 256 * core, 256), 256)
     twin_cols = pl.ds(pl.multiple_of(512 * zh + 256 * (1 - core), 256), 256)
 
@@ -377,7 +378,7 @@
 
     def fin_copy(i, r0, rows):
         span = pl.ds(r0, rows)
-        return remote(fin_out.at[span], fin_in.at[span], ds.at[CHUNKS + i], dr.at[CHUNKS + i], twin)
+        return remote(fin_out.at[span], fin_in.at[span], ds.at[len(CHUNKS) + i], dr.at[len(CHUNKS) + i], twin)
 
     def send_terms(i, r0, rows):
         fin_out[r0 : r0 + rows, :] = terms(r0, rows, twin_cols).astype(BF16)
@@ -386,14 +387,30 @@
     def finish(i, r0, rows):
         fin_copy(i, r0, rows).wait_recv()
         span = slice(r0, r0 + rows)
-        out[span, :] = (acc[span, 0:256] + 0.5 * fin_in[span, :].astype(F32)).astype(BF16)
+        out[span, :] = (x2[span, :] + 0.5 * fin_in[span, :].astype(F32)).astype(BF16)
 
     def own_terms(r0, rows):
-        acc[r0 : r0 + rows, 0:256] = x1[r0 : r0 + rows, my_cols] + 0.5 * terms(r0, rows, my_cols)
-
-    attend_some(1, 4, 2, range(4))
+        span = slice(r0, r0 + rows)
+        x_new = st[span, my_cols].astype(F32) + 0.5 * (acc[span, my_cols] + pv_in[span, my_cols].astype(F32))
+        x2[span, :] = x_new + 0.5 * terms(r0, rows, my_cols)
+
+    attend([TILE * t for t in range(1, 9)], (2, 3))
     send_terms(0, *INNER)
     own_terms(*INNER)
+    for s in range(PARTS):
+
+
+        @pl.when(outer)
+        def _():
+            z_copy(s).wait_send()
+            z_forward(s).wait_send()
+
+        for j in range(2):
+            x_copy(s, j, colour).wait_send()
+            y_copy(s, j, colour).wait_send()
+    halo_left(first_halo + id_copies)
+    for i in range(len(CHUNKS)):
+        pv_copy(i).wait_send()
     halo_arrived(second_halo)
     for w, pair in ((wq, 0), (fq, 2)):
         keys(h2, w, pair, True)
@@ -401,25 +418,13 @@
     attend((0, (TILES - 1) * TILE), range(4))
     send_terms(1, *FIRST)
     send_terms(2, *LAST)
+    finish(0, *INNER)
     own_terms(*FIRST)
     own_terms(*LAST)
-    for i, span in enumerate((INNER, FIRST, LAST)):
-        finish(i, *span)
-
-    for s in range(PARTS):
-
-
-        @pl.when(outer)
-        def _():
-            z_copy(s).wait_send()
-            z_forward(s).wait_send()
-
-        for j in range(2):
-            x_copy(s, j, colour).wait_send()
-            y_copy(s, j, colour).wait_send()
-    halo_left(first_halo + id_copies + second_halo)
-    for r in range(CHUNKS):
-        pv_copy(r).wait_send()
+    finish(1, *FIRST)
+    finish(2, *LAST)
+
+    halo_left(second_halo)
     for i, span in enumerate((INNER, FIRST, LAST)):
         fin_copy(i, *span).wait_send()
 
@@ -458,7 +463,7 @@
             pltpu.VMEM((ROWS, D), F32),
             pltpu.VMEM((ROWS, D), BF16),
             pltpu.VMEM((ROWS, D), BF16),
-            pltpu.VMEM((ROWS, D), F32),
+            pltpu.VMEM((ROWS, 256), F32),
             pltpu.VMEM((ROWS, 256), BF16),
             pltpu.VMEM((ROWS, 256), BF16),
             dma((7,)),
@@ -471,8 +476,8 @@
             dma((2 * PARTS,)),
             dma((6,)),
             dma((6,)),
-            dma((CHUNKS + 3,)),
-            dma((CHUNKS + 3,)),
+            dma((len(CHUNKS) + 3,)),
+            dma((len(CHUNKS) + 3,)),
         ],
         compiler_params=pltpu.CompilerParams(
             collective_id=0, has_side_effects=True, vmem_limit_bytes=62 << 20

time: 46.5 us -> 46 us (0.989)
  the two profiles are of different devices: /device:TPU:49 before, /device:TPU:71 now
where the time goes in v3:
time: 46 us; the launch traced here: 45.9 us
  Pallas kernels  44.2 us (96%)
  local copies, waits for them, and re-layouts  1.65 us (4%)
    pallas_call x1, Pallas kernels, shards(): pl.pallas_call(kernel, out_shape=jax.ShapeDtypeStruct((ROWS, 256), BF16),...  44.2 us
    unnamed x1, local copies, waits for them, and re-layouts  1.65 us

profile of v3, /device:TPU:71, one launch (start us, length us, event | category | flops | bytes accessed | tf_op | source)
XLA Modules:
  0.0 45.9 jit_solution(13478404384293896985)
XLA Ops:
  0.0 44.2 %decoder.1 = bf16[480,256]{1,0:T(8,128)(2,1)} custom-call(bf16[480,1024]{1,0:T(8,128)(2,1)} %state_h.1, bf16[480,1024]{1,0:T(8,128)(2,1)} %cond_h.1, bf16[3,1024,256]{2,1,0:T(8,128)(2,1)} %wqkv_h.1, bf16[256,1024]{1,0:T(8,128)(2,1)} %wout_h.1, bf16[1024]{0:T(1024)(128)(2,1)} %tvec_h.1, bf16[1024]{0:T(1024)(128)(2,1)} %gain_h.1, s32[480]{0:T(512)} %ids_h.1), custom_call_target="tpu_custom_call" | custom-call | flops 4499999744 | bytes 4500000 | tf_op jit(solution)/shard_map/decoder/pallas_call | solution.py:436
  44.2 1.7 %copy.9 = bf16[480,256]{1,0:T(8,128)(2,1)} copy(bf16[480,256]{1,0:T(8,128)(2,1)} %decoder.1) | data formatting | bytes 491520

commit v4 on v3

--- a/solution.py
+++ b/solution.py
@@ -18,7 +18,7 @@
 KEYS = 128
 TILES = ROWS // TILE
 LANES = 640
-CHUNKS = ((ROWS - 48, 48), (0, 48)) + tuple((r, 96) for r in range(48, ROWS - 48, 96))
+CHUNKS = ((ROWS - 48, 48), (0, 48)) + tuple((r, 192) for r in range(48, ROWS - 48, 192))
 PARTS = 8
 
 

time: 46 us -> 46 us (level)
  no operation moved by 1% of the time
where the time goes in v4:
time: 46 us; the launch traced here: 45.8 us
  Pallas kernels  44.2 us (96%)
  local copies, waits for them, and re-layouts  1.65 us (4%)
    pallas_call x1, Pallas kernels, shards(): pl.pallas_call(kernel, out_shape=jax.ShapeDtypeStruct((ROWS, 256), BF16),...  44.2 us
    unnamed x1, local copies, waits for them, and re-layouts  1.65 us

profile of v4, /device:TPU:71, one launch (start us, length us, event | category | flops | bytes accessed | tf_op | source)
XLA Modules:
  0.0 45.8 jit_solution(13926715306210198514)
XLA Ops:
  0.0 44.2 %decoder.1 = bf16[480,256]{1,0:T(8,128)(2,1)} custom-call(bf16[480,1024]{1,0:T(8,128)(2,1)} %state_h.1, bf16[480,1024]{1,0:T(8,128)(2,1)} %cond_h.1, bf16[3,1024,256]{2,1,0:T(8,128)(2,1)} %wqkv_h.1, bf16[256,1024]{1,0:T(8,128)(2,1)} %wout_h.1, bf16[1024]{0:T(1024)(128)(2,1)} %tvec_h.1, bf16[1024]{0:T(1024)(128)(2,1)} %gain_h.1, s32[480]{0:T(512)} %ids_h.1), custom_call_target="tpu_custom_call" | custom-call | flops 4499999744 | bytes 4500000 | tf_op jit(solution)/shard_map/decoder/pallas_call | solution.py:436
  44.2 1.7 %copy.9 = bf16[480,256]{1,0:T(8,128)(2,1)} copy(bf16[480,256]{1,0:T(8,128)(2,1)} %decoder.1) | data formatting | bytes 491520
